TPU v7x, 32 devices: a whole 2x2x4 slice. The times are simulated.
32 devices in a mesh: cases: 2 (over y), tm: 4 (over z), region: 4 (over x, core).
Axes of the slice: x: 2, y: 2, z: 4, core: 2. Of those that a mesh axis runs over, the one named last changes fastest.
Arguments:
- former_estimate: float32 [384, 32, 128], P(('cases', 'tm'), 'region'), parts along dimension 0, may hold values from -6 to 6
- excitation: bfloat16 [384, 32, 128], P(('cases', 'tm'), 'region'), parts along dimension 0, may hold values from -6 to 6
- susceptance_maps: bfloat16 [32, 4, 128, 128], P('region'), may hold values from -0.125 to 0.125
- linked_partner_target: int32 [32, 4], P('region'), may hold values from 0 to 31, as said below
- attenuation: float32 [32, 64], P('region'), may hold values from 0.0002 to 0.03
- revolution_angle: float32 [32, 64], P('region'), may hold values from -0.6 to 0.6
- saturated_flag: int32 [64, 64], P(('cases', 'region')), parts along dimension 0, may hold values 0 or 1
- gain_surge: float32 [384], P(('cases', 'tm')), parts along dimension 0, may hold values from 0.25 to 1
Outputs:
- waveform: float32 [384, 32, 128], P(('cases', 'tm'), 'region'), parts along dimension 0
There are 2 independent parts, one for each index of `cases`. A program takes and returns all parts, laid end to end along the dimension named above; an argument that names none is the same for every part. Nothing has to cross between parts.
Inputs may be any that keep to these rules, and one draw needn't show every extreme that they name: `linked_partner_target`: block row b lies in region g = b // 8. Its column 0 is b itself, column 1 a block of region g, column 2 one of the last 4 blocks of region g - 1 and column 3 one of the first 4 blocks of region g + 1, regions counted around a cycle of 32 // 8.
All inputs are finite; a program needn't handle non-finite values. No bound on the sum of `saturated_flag` on one device may be relied on, other than what follows from the above.
Results may differ from a plain program's by a relative error of at most 0.0017.
Values may be sent and summed in bfloat16 or wider, within the bound.
A program may use at most 64 MiB of HBM per device.

v0:
```python
import jax
import jax.numpy as jnp
from jax import lax
from jax.sharding import PartitionSpec as P

BND = 4
SWEEPS = 3
clip_level = 0.5


def with_halo(block, sides, width):
    for axis, dim in sides:
        count = lax.axis_size(axis)
        forward = [(i, i + 1) for i in range(count - 1)]
        forward.append((count - 1, 0))
        backward = [(target, source) for source, target in forward]
        low = lax.ppermute(
            lax.slice_in_dim(block, block.shape[dim] - width, None, axis=dim), axis, forward
        )
        high = lax.ppermute(lax.slice_in_dim(block, 0, width, axis=dim), axis, backward)
        block = jnp.concatenate([low, block, high], axis=dim)
    return block


def complex_mul(first, second):
    half = first.shape[-1] // 2
    first_re, first_im = (first[..., :half], first[..., half:])
    second_re, second_im = (second[..., :half], second[..., half:])
    return jnp.concatenate(
        [first_re * second_re - first_im * second_im, first_re * second_im + first_im * second_re],
        axis=-1,
    )


def combine(early, late):
    return (complex_mul(late[0], early[0]), complex_mul(late[0], early[1]) + late[1])


def bus_terms(attenuation, revolution_angle):
    modulus = jnp.exp(-attenuation)
    cosine = modulus * jnp.cos(revolution_angle)
    sine = modulus * jnp.sin(revolution_angle)
    argument_spin = jnp.concatenate([cosine, sine], axis=-1)
    input_gain = jnp.sqrt((1.0 - cosine) ** 2 + sine**2)
    return (argument_spin, jnp.concatenate([input_gain, input_gain], axis=-1))


def limit_current(current, saturated_flag):
    half = current.shape[-1] // 2
    square = current[..., :half] ** 2 + current[..., half:] ** 2
    scaling_factor = jnp.where(
        saturated_flag == 1, clip_level / jnp.sqrt(clip_level**2 + square), 1.0
    )
    return current * jnp.concatenate([scaling_factor, scaling_factor], axis=-1)


def periodic_end(total_a, total_b):
    half = total_a.shape[-1] // 2
    denom_re = 1.0 - total_a[..., :half]
    denom_im = -total_a[..., half:]
    square = denom_re**2 + denom_im**2
    conjugate = jnp.concatenate([denom_re / square, -denom_im / square], axis=-1)
    return complex_mul(total_b, conjugate)


def local(
    former_estimate,
    excitation,
    susceptance_maps,
    linked_partner_target,
    attenuation,
    revolution_angle,
    saturated_flag,
    gain_surge,
):
    blocks = former_estimate.shape[1]
    buses = attenuation.shape[1]
    argument_spin, input_gain = bus_terms(attenuation, revolution_angle)
    incremental_spin = gain_surge[:, None, None] * argument_spin[None]
    drive_base = excitation.astype(jnp.float32)
    region_index = lax.axis_index("region")
    network = blocks * lax.axis_size("region")
    local_col = (linked_partner_target - region_index * blocks) % network
    local_col = jnp.where(local_col >= network - BND, local_col - network, local_col) + BND
    unit = jnp.concatenate(
        [jnp.ones((blocks, buses), jnp.float32), jnp.zeros((blocks, buses), jnp.float32)], axis=-1
    )
    nothing = jnp.zeros((blocks, 2 * buses), jnp.float32)
    wave = former_estimate
    for sweep_index in range(SWEEPS):
        rounded = wave.astype(jnp.bfloat16)
        extended = with_halo(rounded, (("region", 1),), BND)
        picked = extended[:, local_col, :]
        current = jnp.einsum(
            "tbkj,bkij->tbi", picked, susceptance_maps, preferred_element_type=jnp.float32
        )
        drive = input_gain[None] * (drive_base - limit_current(current, saturated_flag[None]))
        local_a, local_b = lax.associative_scan(combine, (incremental_spin, drive), axis=0)
        own_map = (local_a[-1], local_b[-1])
        every_a, every_b = (
            lax.all_gather(own_map[0][None], "tm", axis=0, tiled=True),
            lax.all_gather(own_map[1][None], "tm", axis=0, tiled=True),
        )
        run_a, run_b = lax.associative_scan(combine, (every_a, every_b), axis=0)
        total_a, total_b = (run_a[-1], run_b[-1])
        time_index = lax.axis_index("tm")
        earlier = jnp.maximum(time_index - 1, 0)
        prior_a = lax.dynamic_index_in_dim(run_a, earlier, 0, keepdims=False)
        prior_b = lax.dynamic_index_in_dim(run_b, earlier, 0, keepdims=False)
        before = (
            jnp.where(time_index > 0, prior_a, unit),
            jnp.where(time_index > 0, prior_b, nothing),
        )
        end_state = periodic_end(total_a, total_b)
        start_state = complex_mul(before[0], end_state) + before[1]
        wave = complex_mul(local_a, start_state[None]) + local_b
    return wave


def solution(mesh):
    in_specs = (
        P(("cases", "tm"), "region", None),
        P(("cases", "tm"), "region", None),
        P("region", None, None, None),
        P("region", None),
        P("region", None),
        P("region", None),
        P(("cases", "region"), None),
        P(("cases", "tm")),
    )
    out_specs = P(("cases", "tm"), "region", None)
    return jax.shard_map(local, mesh=mesh, in_specs=in_specs, out_specs=out_specs, check_vma=False)
```

profile of v0, /device:TPU:0, one launch (start us, length us, event | category | flops | bytes accessed | tf_op | source)
XLA Modules:
  0.0 90.0 jit_solution(5454847663768018754)
XLA Ops:
  0.0 1.1 %copy.114 = bf16[48,8,128]{2,0,1:T(8,128)(2,1)S(1)} copy(f32[48,8,128]{2,1,0:T(8,128)} %param.8) | data formatting | bytes 294912 | tf_op args[0]
  1.1 0.5 collective-permute-start
  1.6 2.0 %collective-permute-start.1 = (bf16[48,4,128]{2,0,1:T(8,128)(2,1)S(1)}, bf16[48,4,128]{2,0,1:T(8,128)(2,1)S(1)}, u32[]{:S(2)}, u32[]{:S(2)}) collective-permute-start(bf16[48,4,128]{2,0,1:T(8,128)(2,1)S(1)} %get-tuple-element.68), channel_id=1, source_target_pairs={{1,0},{2,1},{3,2},{0,3},{5,4},{6,5},{7,6},{4,7},{9,8},{10,9},{11,1... | collective-permute-start | bytes 147464 | tf_op jit(solution)/shard_map/ppermute | solution.py:20
  3.6 0.7 copy-done.9
  4.5 0.5 copy-done.5
  5.1 0.7 copy-done.10
  5.9 0.6 copy-done.1
  6.6 0.6 gather_fusion
  8.0 0.7 copy-done.2
  12.4 0.5 slice-done
  13.4 14.1 %all_gather.14 = f32[4,8,128]{2,1,0:T(8,128)S(1)} all-gather(f32[1,8,128]{2,1,0:T(8,128)S(1)} %slice_add_fusion.40), channel_id=1, replica_groups=mesh['cases'=2,'tm'=4,'region'=4] {'tm'}, dimensions={0}, use_global_device_ids=true | all-gather | bytes 20480 | tf_op jit(solution)/shard_map/all_gather | solution.py:101
  28.5 13.1 %all_gather.15 = f32[4,8,128]{2,1,0:T(8,128)S(1)} all-gather(f32[1,8,128]{2,1,0:T(8,128)S(1)} %slice_add_fusion.37), channel_id=1, replica_groups=mesh['cases'=2,'tm'=4,'region'=4] {'tm'}, dimensions={0}, use_global_device_ids=true | all-gather | bytes 20480 | tf_op jit(solution)/shard_map/all_gather | solution.py:102
  42.3 0.7 slice-done.1
  43.0 0.7 copy-done.7
  44.5 1.7 %collective-permute-start.3 = (bf16[48,4,128]{2,1,0:T(4,128)(2,1)S(1)}, bf16[48,4,128]{2,1,0:T(4,128)(2,1)S(1)}, u32[]{:S(2)}, u32[]{:S(2)}) collective-permute-start(bf16[48,4,128]{2,1,0:T(4,128)(2,1)S(1)} %get-tuple-element.62), channel_id=1, source_target_pairs={{1,0},{2,1},{3,2},{0,3},{5,4},{6,5},{7,6},{4,7},{9,8},{10,9},{11,1... | collective-permute-start | bytes 147464 | tf_op jit(solution)/shard_map/ppermute | solution.py:20
  46.2 1.8 %collective-permute-done.2 = bf16[48,4,128]{2,1,0:T(4,128)(2,1)S(1)} collective-permute-done((bf16[48,4,128]{2,1,0:T(4,128)(2,1)S(1)}, bf16[48,4,128]{2,1,0:T(4,128)(2,1)S(1)}, u32[]{:S(2)}, u32[]{:S(2)}) %collective-permute-start.2) | collective-permute-done | bytes 49184 | tf_op jit(solution)/shard_map/ppermute | solution.py:17
  48.2 0.6 gather_fusion.1
  52.4 13.1 %all_gather.16 = f32[4,8,128]{2,1,0:T(8,128)S(1)} all-gather(f32[1,8,128]{2,1,0:T(8,128)S(1)} %slice_add_fusion.32), channel_id=1, replica_groups=mesh['cases'=2,'tm'=4,'region'=4] {'tm'}, dimensions={0}, use_global_device_ids=true | all-gather | bytes 20480 | tf_op jit(solution)/shard_map/all_gather | solution.py:102
  65.8 0.6 copy-done.4
  67.3 1.7 %collective-permute-start.5 = (bf16[48,4,128]{2,1,0:T(4,128)(2,1)S(1)}, bf16[48,4,128]{2,1,0:T(4,128)(2,1)S(1)}, u32[]{:S(2)}, u32[]{:S(2)}) collective-permute-start(bf16[48,4,128]{2,1,0:T(4,128)(2,1)S(1)} %get-tuple-element.58), channel_id=1, source_target_pairs={{1,0},{2,1},{3,2},{0,3},{5,4},{6,5},{7,6},{4,7},{9,8},{10,9},{11,1... | collective-permute-start | bytes 147464 | tf_op jit(solution)/shard_map/ppermute | solution.py:20
  69.0 1.8 %collective-permute-done.4 = bf16[48,4,128]{2,1,0:T(4,128)(2,1)S(1)} collective-permute-done((bf16[48,4,128]{2,1,0:T(4,128)(2,1)S(1)}, bf16[48,4,128]{2,1,0:T(4,128)(2,1)S(1)}, u32[]{:S(2)}, u32[]{:S(2)}) %collective-permute-start.4) | collective-permute-done | bytes 49184 | tf_op jit(solution)/shard_map/ppermute | solution.py:17
  70.9 0.6 gather_fusion.2
  75.2 13.1 %all_gather.17 = f32[4,8,128]{2,1,0:T(8,128)S(1)} all-gather(f32[1,8,128]{2,1,0:T(8,128)S(1)} %slice_add_fusion.27), channel_id=1, replica_groups=mesh['cases'=2,'tm'=4,'region'=4] {'tm'}, dimensions={0}, use_global_device_ids=true | all-gather | bytes 20480 | tf_op jit(solution)/shard_map/all_gather | solution.py:102
  89.2 0.8 maximum_add_fusion.2
  (290 shorter events, 16.2 us)
Async XLA Ops:
  0.0 7.3 %copy-start = (bf16[8,4,128,128]{3,2,1,0:T(8,128)(2,1)S(1)}, bf16[8,4,128,128]{3,2,1,0:T(8,128)(2,1)}, u32[]{:S(2)}) copy-start(bf16[8,4,128,128]{3,2,1,0:T(8,128)(2,1)} %param.10) | copy-start | bytes 3145732
  1.1 2.5 %copy-start.8 = (s32[8,64]{1,0:T(8,128)S(1)}, s32[8,64]{1,0:T(8,128)}, u32[]{:S(2)}) copy-start(s32[8,64]{1,0:T(8,128)} %param.14) | copy-start | bytes 6148
  1.1 5.5 %collective-permute-start = (bf16[48,4,128]{2,0,1:T(8,128)(2,1)S(1)}, bf16[48,4,128]{2,0,1:T(8,128)(2,1)S(1)}, u32[]{:S(2)}, u32[]{:S(2)}) collective-permute-start(bf16[48,4,128]{2,0,1:T(8,128)(2,1)S(1)} %get-tuple-element.67), channel_id=1, source_target_pairs={{0,1},{1,2},{2,3},{3,0},{4,5},{5,6},{6,7},{7,4},{8,9},{9,10},{10,1... | collective-permute-start | bytes 147464 | tf_op jit(solution)/shard_map/ppermute | solution.py:17
  1.6 5.0 %collective-permute-start.1 = (bf16[48,4,128]{2,0,1:T(8,128)(2,1)S(1)}, bf16[48,4,128]{2,0,1:T(8,128)(2,1)S(1)}, u32[]{:S(2)}, u32[]{:S(2)}) collective-permute-start(bf16[48,4,128]{2,0,1:T(8,128)(2,1)S(1)} %get-tuple-element.68), channel_id=1, source_target_pairs={{1,0},{2,1},{3,2},{0,3},{5,4},{6,5},{7,6},{4,7},{9,8},{10,9},{11,1... | collective-permute-start | bytes 147464 | tf_op jit(solution)/shard_map/ppermute | solution.py:20
  3.6 0.7 copy-start.9
  4.3 0.7 copy-start.5
  4.3 0.7 copy-start.6
  5.1 0.7 copy-start.10
  5.9 0.7 copy-start.1
  7.8 0.9 copy-start.2
  12.2 0.7 slice-start
  27.5 14.5 %copy-start.3 = (f32[4,8,128]{2,1,0:T(8,128)}, f32[4,8,128]{2,1,0:T(8,128)S(1)}, u32[]{:S(2)}) copy-start(f32[4,8,128]{2,1,0:T(8,128)S(1)} %all_gather.14) | copy-start | bytes 49156
  42.3 0.7 slice-start.1
  43.0 0.7 copy-start.7
  44.4 3.6 %collective-permute-start.2 = (bf16[48,4,128]{2,1,0:T(4,128)(2,1)S(1)}, bf16[48,4,128]{2,1,0:T(4,128)(2,1)S(1)}, u32[]{:S(2)}, u32[]{:S(2)}) collective-permute-start(bf16[48,4,128]{2,1,0:T(4,128)(2,1)S(1)} %get-tuple-element.61), channel_id=1, source_target_pairs={{0,1},{1,2},{2,3},{3,0},{4,5},{5,6},{6,7},{7,4},{8,9},{9,10},{10,1... | collective-permute-start | bytes 147464 | tf_op jit(solution)/shard_map/ppermute | solution.py:17
  44.5 3.5 %collective-permute-start.3 = (bf16[48,4,128]{2,1,0:T(4,128)(2,1)S(1)}, bf16[48,4,128]{2,1,0:T(4,128)(2,1)S(1)}, u32[]{:S(2)}, u32[]{:S(2)}) collective-permute-start(bf16[48,4,128]{2,1,0:T(4,128)(2,1)S(1)} %get-tuple-element.62), channel_id=1, source_target_pairs={{1,0},{2,1},{3,2},{0,3},{5,4},{6,5},{7,6},{4,7},{9,8},{10,9},{11,1... | collective-permute-start | bytes 147464 | tf_op jit(solution)/shard_map/ppermute | solution.py:20
  65.7 0.7 copy-start.4
  67.2 3.6 %collective-permute-start.4 = (bf16[48,4,128]{2,1,0:T(4,128)(2,1)S(1)}, bf16[48,4,128]{2,1,0:T(4,128)(2,1)S(1)}, u32[]{:S(2)}, u32[]{:S(2)}) collective-permute-start(bf16[48,4,128]{2,1,0:T(4,128)(2,1)S(1)} %get-tuple-element.57), channel_id=1, source_target_pairs={{0,1},{1,2},{2,3},{3,0},{4,5},{5,6},{6,7},{7,4},{8,9},{9,10},{10,1... | collective-permute-start | bytes 147464 | tf_op jit(solution)/shard_map/ppermute | solution.py:17
  67.3 3.5 %collective-permute-start.5 = (bf16[48,4,128]{2,1,0:T(4,128)(2,1)S(1)}, bf16[48,4,128]{2,1,0:T(4,128)(2,1)S(1)}, u32[]{:S(2)}, u32[]{:S(2)}) collective-permute-start(bf16[48,4,128]{2,1,0:T(4,128)(2,1)S(1)} %get-tuple-element.58), channel_id=1, source_target_pairs={{1,0},{2,1},{3,2},{0,3},{5,4},{6,5},{7,6},{4,7},{9,8},{10,9},{11,1... | collective-permute-start | bytes 147464 | tf_op jit(solution)/shard_map/ppermute | solution.py:20
where the time goes:
time: 90.4 us; the launch traced here: 90 us
  blocking collectives  53.5 us (59%)
  local copies, waits for them, and re-layouts  12.5 us (14%)
  other arithmetic  11.7 us (13%)
  starting transfers between devices  6.07 us (7%)
  waiting for transfers between devices  3.55 us (4%)
  matrix products  1.36 us (2%)
  between operations  1.28 us (1%)
    all_gather x3, blocking collectives, local(): lax.all_gather(own_map[1][None], 'tm', axis=0, tiled=True)  39.4 us
    all_gather x1, blocking collectives, local(): lax.all_gather(own_map[0][None], 'tm', axis=0, tiled=True)  14.1 us
    unnamed x26, local copies, waits for them, and re-layouts  5.99 us
    ppermute x3, starting transfers between devices, with_halo(): lax.ppermute(lax.slice_in_dim(block, 0, width, axis=dim), axis, backward)  5.45 us
    sub x45, other arithmetic, complex_mul(): first_re * second_re - first_im * second_im  4.13 us
    ppermute x3, waiting for transfers between devices, with_halo(): lax.ppermute(lax.slice_in_dim(block, block.shape[dim] - width, None, axis...  3.54 us
    add x33, other arithmetic, combine(): complex_mul(late[0], early[1]) + late[1]  2.7 us
    pad x34, local copies, waits for them, and re-layouts, local(): lax.associative_scan(combine, (incremental_spin, drive), axis=0)  2.34 us
  transfers between devices with their start and end apart: 6, of which 2 were waited for; matrix products, arithmetic and copies ran while one was open for 0% of the time, Pallas kernels for 0%

commit v1 on v0

--- a/solution.py
+++ b/solution.py
@@ -6,6 +6,24 @@
 BND = 4
 SWEEPS = 3
 clip_level = 0.5
+
+
+def collect(value, axis, dim):
+    ways, here, step = (lax.axis_size(axis), lax.axis_index(axis), value.shape[dim])
+    lengths = [n * ways if d == dim else n for d, n in enumerate(value.shape)]
+    full = lax.dynamic_update_slice_in_dim(
+        jnp.zeros(lengths, value.dtype), value, here * step, axis=dim
+    )
+    going_up = going_down = value
+    for far in range(1, ways // 2 + 1):
+        going_up = lax.ppermute(going_up, axis, [(d, (d + 1) % ways) for d in range(ways)])
+        full = lax.dynamic_update_slice_in_dim(full, going_up, (here - far) % ways * step, axis=dim)
+        if 2 * far < ways:
+            going_down = lax.ppermute(going_down, axis, [(d, (d - 1) % ways) for d in range(ways)])
+            full = lax.dynamic_update_slice_in_dim(
+                full, going_down, (here + far) % ways * step, axis=dim
+            )
+    return full
 
 
 def with_halo(block, sides, width):
@@ -98,7 +116,7 @@
         local_a, local_b = lax.associative_scan(combine, (incremental_spin, drive), axis=0)
         own_map = (local_a[-1], local_b[-1])
         every_a, every_b = (
-            lax.all_gather(own_map[0][None], "tm", axis=0, tiled=True),
+            collect(own_map[0][None], "tm", 0),
             lax.all_gather(own_map[1][None], "tm", axis=0, tiled=True),
         )
         run_a, run_b = lax.associative_scan(combine, (every_a, every_b), axis=0)

time: 90.4 us -> 84.8 us (0.938)
  blocking collectives: 53.5 us -> 39.4 us
  waiting for transfers between devices: 3.55 us -> 8.78 us
  starting transfers between devices: 6.07 us -> 10.7 us
  local copies, waits for them, and re-layouts: 12.5 us -> 11.1 us
    all_gather x1 -> x0, blocking collectives: 14.1 us -> none  [local(): lax.all_gather(own_map[0][None], 'tm', axis=0, tiled=True)]
    ppermute x0 -> x3, waiting for transfers between devices: none -> 5.23 us  [the longest x2 5.23 us: collect(): lax.ppermute(going_up, axis, [(d, (d + 1) % ways) for d in range(ways)])]
    ppermute x0 -> x3, starting transfers between devices: none -> 4.64 us  [the longest x2 2.55 us: collect(): lax.ppermute(going_up, axis, [(d, (d + 1) % ways) for d in range(ways)])]
    unnamed x26 -> x22, local copies, waits for them, and re-layouts: 5.99 us -> 5.28 us
  transfers between devices with their start and end apart: 6 -> 9, of which waited for: 2 -> 3; matrix products, arithmetic and copies ran while one was open for 0% -> 2% of each run, Pallas kernels for 0% -> 0%
where the time goes in v1:
time: 84.8 us; the launch traced here: 84.4 us
  blocking collectives  39.4 us (46%)
  other arithmetic  11.8 us (14%)
  local copies, waits for them, and re-layouts  11.1 us (13%)
  starting transfers between devices  10.7 us (13%)
  waiting for transfers between devices  8.78 us (10%)
  matrix products  1.36 us (2%)
  between operations  1.35 us (2%)
    all_gather x3, blocking collectives, local(): lax.all_gather(own_map[1][None], 'tm', axis=0, tiled=True)  39.4 us
    ppermute x3, starting transfers between devices, with_halo(): lax.ppermute(lax.slice_in_dim(block, 0, width, axis=dim), axis, backward)  5.45 us
    unnamed x22, local copies, waits for them, and re-layouts  5.28 us
    ppermute x2, waiting for transfers between devices, collect(): lax.ppermute(going_up, axis, [(d, (d + 1) % ways) for d in range(ways)])  5.23 us
    sub x45, other arithmetic, complex_mul(): first_re * second_re - first_im * second_im  4.14 us
    ppermute x3, waiting for transfers between devices, with_halo(): lax.ppermute(lax.slice_in_dim(block, block.shape[dim] - width, None, axis...  3.54 us
    add x33, other arithmetic, combine(): complex_mul(late[0], early[1]) + late[1]  2.7 us
    ppermute x2, starting transfers between devices, collect(): lax.ppermute(going_up, axis, [(d, (d + 1) % ways) for d in range(ways)])  2.55 us
  transfers between devices with their start and end apart: 9, of which 3 were waited for; matrix products, arithmetic and copies ran while one was open for 2% of the time, Pallas kernels for 0%

profile of v1, /device:TPU:0, one launch (start us, length us, event | category | flops | bytes accessed | tf_op | source)
XLA Modules:
  0.0 84.4 jit_solution(15359029266268801044)
XLA Ops:
  0.0 1.1 %copy.117 = bf16[48,8,128]{2,0,1:T(8,128)(2,1)S(1)} copy(f32[48,8,128]{2,1,0:T(8,128)} %param.8) | data formatting | bytes 294912 | tf_op args[0]
  1.1 0.5 collective-permute-start.3
  1.6 2.0 %collective-permute-start.4 = (bf16[48,4,128]{2,0,1:T(8,128)(2,1)S(1)}, bf16[48,4,128]{2,0,1:T(8,128)(2,1)S(1)}, u32[]{:S(2)}, u32[]{:S(2)}) collective-permute-start(bf16[48,4,128]{2,0,1:T(8,128)(2,1)S(1)} %get-tuple-element.70), channel_id=1, source_target_pairs={{1,0},{2,1},{3,2},{0,3},{5,4},{6,5},{7,6},{4,7},{9,8},{10,9},{11,1... | collective-permute-start | bytes 147464 | tf_op jit(solution)/shard_map/ppermute | solution.py:38
  3.6 0.7 copy-done.7
  4.5 0.5 copy-done.3
  5.1 0.7 copy-done.8
  6.0 0.6 copy-done.1
  6.6 0.6 gather_fusion
  8.0 0.7 copy-done.2
  12.4 0.5 slice-done
  13.4 2.4 %collective-permute-start = (f32[1,8,128]{2,1,0:T(8,128)S(1)}, f32[1,8,128]{2,1,0:T(8,128)S(1)}, u32[]{:S(2)}, u32[]{:S(2)}) collective-permute-start(f32[1,8,128]{2,1,0:T(8,128)S(1)} %get-tuple-element.20), channel_id=1, source_target_pairs={{0,4},{4,8},{8,12},{12,0},{1,5},{5,9},{9,13},{13,1},{2,6},{6,10},{... | collective-permute-start | bytes 12296 | tf_op jit(solution)/shard_map/ppermute | solution.py:19
  15.8 2.1 %collective-permute-start.1 = (f32[1,8,128]{2,1,0:T(8,128)S(1)}, f32[1,8,128]{2,1,0:T(8,128)S(1)}, u32[]{:S(2)}, u32[]{:S(2)}) collective-permute-start(f32[1,8,128]{2,1,0:T(8,128)S(1)} %get-tuple-element.20), channel_id=1, source_target_pairs={{0,12},{4,0},{8,4},{12,8},{1,13},{5,1},{9,5},{13,9},{2,14},{6,2},{... | collective-permute-start | bytes 12296 | tf_op jit(solution)/shard_map/ppermute | solution.py:22
  18.9 13.1 %all_gather.9 = f32[4,8,128]{2,1,0:T(8,128)S(1)} all-gather(f32[1,8,128]{2,1,0:T(8,128)S(1)} %slice_add_fusion.37), channel_id=1, replica_groups=mesh['cases'=2,'tm'=4,'region'=4] {'tm'}, dimensions={0}, use_global_device_ids=true | all-gather | bytes 20480 | tf_op jit(solution)/shard_map/all_gather | solution.py:120
  32.2 5.2 %collective-permute-done.2 = f32[1,8,128]{2,1,0:T(8,128)S(1)} collective-permute-done((f32[1,8,128]{2,1,0:T(8,128)S(1)}, f32[1,8,128]{2,1,0:T(8,128)S(1)}, u32[]{:S(2)}, u32[]{:S(2)}) %collective-permute-start.2) | collective-permute-done | bytes 4128 | tf_op jit(solution)/shard_map/ppermute | solution.py:19
  38.2 0.7 copy-done.5
  39.6 1.7 %collective-permute-start.6 = (bf16[48,4,128]{2,1,0:T(4,128)(2,1)S(1)}, bf16[48,4,128]{2,1,0:T(4,128)(2,1)S(1)}, u32[]{:S(2)}, u32[]{:S(2)}) collective-permute-start(bf16[48,4,128]{2,1,0:T(4,128)(2,1)S(1)} %get-tuple-element.64), channel_id=1, source_target_pairs={{1,0},{2,1},{3,2},{0,3},{5,4},{6,5},{7,6},{4,7},{9,8},{10,9},{11,1... | collective-permute-start | bytes 147464 | tf_op jit(solution)/shard_map/ppermute | solution.py:38
  41.3 1.8 %collective-permute-done.5 = bf16[48,4,128]{2,1,0:T(4,128)(2,1)S(1)} collective-permute-done((bf16[48,4,128]{2,1,0:T(4,128)(2,1)S(1)}, bf16[48,4,128]{2,1,0:T(4,128)(2,1)S(1)}, u32[]{:S(2)}, u32[]{:S(2)}) %collective-permute-start.5) | collective-permute-done | bytes 49184 | tf_op jit(solution)/shard_map/ppermute | solution.py:35
  43.3 0.6 gather_fusion.1
  47.5 13.1 %all_gather.10 = f32[4,8,128]{2,1,0:T(8,128)S(1)} all-gather(f32[1,8,128]{2,1,0:T(8,128)S(1)} %slice_add_fusion.32), channel_id=1, replica_groups=mesh['cases'=2,'tm'=4,'region'=4] {'tm'}, dimensions={0}, use_global_device_ids=true | all-gather | bytes 20480 | tf_op jit(solution)/shard_map/all_gather | solution.py:120
  61.7 1.7 %collective-permute-start.8 = (bf16[48,4,128]{2,1,0:T(4,128)(2,1)S(1)}, bf16[48,4,128]{2,1,0:T(4,128)(2,1)S(1)}, u32[]{:S(2)}, u32[]{:S(2)}) collective-permute-start(bf16[48,4,128]{2,1,0:T(4,128)(2,1)S(1)} %get-tuple-element.60), channel_id=1, source_target_pairs={{1,0},{2,1},{3,2},{0,3},{5,4},{6,5},{7,6},{4,7},{9,8},{10,9},{11,1... | collective-permute-start | bytes 147464 | tf_op jit(solution)/shard_map/ppermute | solution.py:38
  63.5 1.8 %collective-permute-done.7 = bf16[48,4,128]{2,1,0:T(4,128)(2,1)S(1)} collective-permute-done((bf16[48,4,128]{2,1,0:T(4,128)(2,1)S(1)}, bf16[48,4,128]{2,1,0:T(4,128)(2,1)S(1)}, u32[]{:S(2)}, u32[]{:S(2)}) %collective-permute-start.7) | collective-permute-done | bytes 49184 | tf_op jit(solution)/shard_map/ppermute | solution.py:35
  65.4 0.6 gather_fusion.2
  69.6 13.1 %all_gather.11 = f32[4,8,128]{2,1,0:T(8,128)S(1)} all-gather(f32[1,8,128]{2,1,0:T(8,128)S(1)} %slice_add_fusion.27), channel_id=1, replica_groups=mesh['cases'=2,'tm'=4,'region'=4] {'tm'}, dimensions={0}, use_global_device_ids=true | all-gather | bytes 20480 | tf_op jit(solution)/shard_map/all_gather | solution.py:120
  83.6 0.8 maximum_add_fusion.2
  (294 shorter events, 16.4 us)
Async XLA Ops:
  0.0 7.3 %copy-start = (bf16[8,4,128,128]{3,2,1,0:T(8,128)(2,1)S(1)}, bf16[8,4,128,128]{3,2,1,0:T(8,128)(2,1)}, u32[]{:S(2)}) copy-start(bf16[8,4,128,128]{3,2,1,0:T(8,128)(2,1)} %param.10) | copy-start | bytes 3145732
  1.1 2.5 %copy-start.6 = (s32[8,64]{1,0:T(8,128)S(1)}, s32[8,64]{1,0:T(8,128)}, u32[]{:S(2)}) copy-start(s32[8,64]{1,0:T(8,128)} %param.14) | copy-start | bytes 6148
  1.1 5.5 %collective-permute-start.3 = (bf16[48,4,128]{2,0,1:T(8,128)(2,1)S(1)}, bf16[48,4,128]{2,0,1:T(8,128)(2,1)S(1)}, u32[]{:S(2)}, u32[]{:S(2)}) collective-permute-start(bf16[48,4,128]{2,0,1:T(8,128)(2,1)S(1)} %get-tuple-element.69), channel_id=1, source_target_pairs={{0,1},{1,2},{2,3},{3,0},{4,5},{5,6},{6,7},{7,4},{8,9},{9,10},{10,1... | collective-permute-start | bytes 147464 | tf_op jit(solution)/shard_map/ppermute | solution.py:35
  1.6 5.0 %collective-permute-start.4 = (bf16[48,4,128]{2,0,1:T(8,128)(2,1)S(1)}, bf16[48,4,128]{2,0,1:T(8,128)(2,1)S(1)}, u32[]{:S(2)}, u32[]{:S(2)}) collective-permute-start(bf16[48,4,128]{2,0,1:T(8,128)(2,1)S(1)} %get-tuple-element.70), channel_id=1, source_target_pairs={{1,0},{2,1},{3,2},{0,3},{5,4},{6,5},{7,6},{4,7},{9,8},{10,9},{11,1... | collective-permute-start | bytes 147464 | tf_op jit(solution)/shard_map/ppermute | solution.py:38
  3.6 0.7 copy-start.7
  4.3 0.7 copy-start.3
  4.3 0.7 copy-start.4
  5.1 0.7 copy-start.8
  5.9 0.7 copy-start.1
  7.8 0.9 %copy-start.2 = (bf16[48,8,128]{2,1,0:T(8,128)(2,1)S(1)}, bf16[48,8,128]{2,1,0:T(8,128)(2,1)}, u32[]{:S(2)}) copy-start(bf16[48,8,128]{2,1,0:T(8,128)(2,1)} %param.9) | copy-start | bytes 294916
  12.2 0.7 slice-start
  13.4 18.6 %collective-permute-start = (f32[1,8,128]{2,1,0:T(8,128)S(1)}, f32[1,8,128]{2,1,0:T(8,128)S(1)}, u32[]{:S(2)}, u32[]{:S(2)}) collective-permute-start(f32[1,8,128]{2,1,0:T(8,128)S(1)} %get-tuple-element.20), channel_id=1, source_target_pairs={{0,4},{4,8},{8,12},{12,0},{1,5},{5,9},{9,13},{13,1},{2,6},{6,10},{... | collective-permute-start | bytes 12296 | tf_op jit(solution)/shard_map/ppermute | solution.py:19
  15.8 16.4 %collective-permute-start.1 = (f32[1,8,128]{2,1,0:T(8,128)S(1)}, f32[1,8,128]{2,1,0:T(8,128)S(1)}, u32[]{:S(2)}, u32[]{:S(2)}) collective-permute-start(f32[1,8,128]{2,1,0:T(8,128)S(1)} %get-tuple-element.20), channel_id=1, source_target_pairs={{0,12},{4,0},{8,4},{12,8},{1,13},{5,1},{9,5},{13,9},{2,14},{6,2},{... | collective-permute-start | bytes 12296 | tf_op jit(solution)/shard_map/ppermute | solution.py:22
  32.0 5.4 %collective-permute-start.2 = (f32[1,8,128]{2,1,0:T(8,128)S(1)}, f32[1,8,128]{2,1,0:T(8,128)S(1)}, u32[]{:S(2)}, u32[]{:S(2)}) collective-permute-start(f32[1,8,128]{2,1,0:T(8,128)S(1)} %collective-permute-done), channel_id=1, source_target_pairs={{0,4},{4,8},{8,12},{12,0},{1,5},{5,9},{9,13},{13,1},{2,6},{6,10},{... | collective-permute-start | bytes 12296 | tf_op jit(solution)/shard_map/ppermute | solution.py:19
  38.1 0.7 copy-start.5
  39.5 3.6 %collective-permute-start.5 = (bf16[48,4,128]{2,1,0:T(4,128)(2,1)S(1)}, bf16[48,4,128]{2,1,0:T(4,128)(2,1)S(1)}, u32[]{:S(2)}, u32[]{:S(2)}) collective-permute-start(bf16[48,4,128]{2,1,0:T(4,128)(2,1)S(1)} %get-tuple-element.63), channel_id=1, source_target_pairs={{0,1},{1,2},{2,3},{3,0},{4,5},{5,6},{6,7},{7,4},{8,9},{9,10},{10,1... | collective-permute-start | bytes 147464 | tf_op jit(solution)/shard_map/ppermute | solution.py:35
  39.6 3.5 %collective-permute-start.6 = (bf16[48,4,128]{2,1,0:T(4,128)(2,1)S(1)}, bf16[48,4,128]{2,1,0:T(4,128)(2,1)S(1)}, u32[]{:S(2)}, u32[]{:S(2)}) collective-permute-start(bf16[48,4,128]{2,1,0:T(4,128)(2,1)S(1)} %get-tuple-element.64), channel_id=1, source_target_pairs={{1,0},{2,1},{3,2},{0,3},{5,4},{6,5},{7,6},{4,7},{9,8},{10,9},{11,1... | collective-permute-start | bytes 147464 | tf_op jit(solution)/shard_map/ppermute | solution.py:38
  61.7 3.6 %collective-permute-start.7 = (bf16[48,4,128]{2,1,0:T(4,128)(2,1)S(1)}, bf16[48,4,128]{2,1,0:T(4,128)(2,1)S(1)}, u32[]{:S(2)}, u32[]{:S(2)}) collective-permute-start(bf16[48,4,128]{2,1,0:T(4,128)(2,1)S(1)} %get-tuple-element.59), channel_id=1, source_target_pairs={{0,1},{1,2},{2,3},{3,0},{4,5},{5,6},{6,7},{7,4},{8,9},{9,10},{10,1... | collective-permute-start | bytes 147464 | tf_op jit(solution)/shard_map/ppermute | solution.py:35
  61.7 3.5 %collective-permute-start.8 = (bf16[48,4,128]{2,1,0:T(4,128)(2,1)S(1)}, bf16[48,4,128]{2,1,0:T(4,128)(2,1)S(1)}, u32[]{:S(2)}, u32[]{:S(2)}) collective-permute-start(bf16[48,4,128]{2,1,0:T(4,128)(2,1)S(1)} %get-tuple-element.60), channel_id=1, source_target_pairs={{1,0},{2,1},{3,2},{0,3},{5,4},{6,5},{7,6},{4,7},{9,8},{10,9},{11,1... | collective-permute-start | bytes 147464 | tf_op jit(solution)/shard_map/ppermute | solution.py:38
